TPU v7x, 32 devices: a whole 2x2x4 slice. The times are simulated.
32 devices in a mesh: seq: 8 (over z, x), head: 4 (over y, core).
Axes of the slice: x: 2, y: 2, z: 4, core: 2. Of those that a mesh axis runs over, the one named last changes fastest.
Arguments:
- query_rows: bfloat16 [4096, 4096], P(('seq', 'head')), may hold values from -6 to 6
- key_rows: bfloat16 [4096, 4096], P(('seq', 'head')), may hold values from -6 to 6
- value_rows: bfloat16 [4096, 4096], P(('seq', 'head')), may hold values from -6 to 6
- write_rate: bfloat16 [4096, 32], P(('seq', 'head')), may hold values from 0 to 1
- log_decay: bfloat16 [4096, 32], P(('seq', 'head')), may hold values from -1.5 to 0
Outputs:
- head_output: bfloat16 [4096, 4096], P(('seq', 'head'))
All inputs are finite; a program needn't handle non-finite values.
Results may differ from a plain program's by a relative error of at most 0.00105.
Values may be sent and summed in bfloat16 or wider, within the bound.
A program may use at most 128 MiB of HBM per device.

v0:
```python
import functools

import jax
import jax.numpy as jnp
from jax import lax
from jax.experimental import pallas as pl
from jax.experimental.pallas import tpu as pltpu
from jax.sharding import PartitionSpec as P

LANES = 128
EPSILON = 1e-06
MESH = pl.DeviceIdType.MESH
F32 = jnp.float32
BF16 = jnp.bfloat16


def halves(x):
    high = x.astype(BF16)
    return high, (x - high.astype(F32)).astype(BF16)


def dot(a, b):
    return jnp.dot(a, b, preferred_element_type=F32)


def dot_t(a, b, dims):
    return lax.dot_general(a, b, (dims, ((), ())), preferred_element_type=F32)


def left3(a):
    high, low = halves(a)
    return jnp.concatenate([high, low, high], axis=1)


def right3(b):
    high, low = halves(b)
    return jnp.concatenate([high, high, low], axis=0)


def dot3(a, b):
    return dot(left3(a), right3(b))


def block_maps(keys, queries, values, beta_col, beta_row, cum_col, cum_row, row, col):
    gram = dot_t(keys, keys, ((1,), (1,)))
    raw_scores = dot_t(queries, keys, ((1,), (1,)))
    diagonal = jnp.where(row == col, gram, 0.0)
    r_col = lax.rsqrt(jnp.sum(diagonal, axis=1, keepdims=True) + EPSILON)
    r_row = lax.rsqrt(jnp.sum(diagonal, axis=0, keepdims=True) + EPSILON)
    within = row >= col
    ratios = jnp.where(within, jnp.exp(jnp.where(within, cum_col - cum_row, 0.0)), 0.0)
    faded = ratios * r_row
    lower = jnp.where(row > col, gram * faded * (beta_col * r_col), 0.0)
    scores = raw_scores * faded
    apart = row ^ col
    inverse = jnp.where(row == col, 1.0, 0.0) - jnp.where(apart == 1, lower, 0.0)
    span = 2
    while span < LANES:
        corner = jnp.where((apart >= span) & (apart < 2 * span), lower, 0.0)
        partial = dot3(corner, inverse)
        inverse = inverse - dot3(inverse, partial)
        span *= 2
    growth_col = jnp.exp(cum_col)
    growth_row = jnp.exp(cum_row)
    end_log = cum_row[:, LANES - 1 :]
    for_values = jnp.concatenate(halves(inverse * beta_row), axis=1)
    for_keys = jnp.concatenate(halves(inverse * (beta_row * growth_row * r_row)), axis=1)
    base = dot(for_values, jnp.concatenate([values, values], axis=0))
    wy = dot(for_keys, jnp.concatenate([keys, keys], axis=0))
    solved = jnp.concatenate([wy, base], axis=1)
    read = dot3(scores, solved)
    carried = solved * (r_col * jnp.exp(end_log - cum_col))
    left = dot_t(
        jnp.concatenate([keys, keys], axis=0),
        jnp.concatenate(halves(carried), axis=0),
        ((0,), (0,)),
    )
    end = jnp.exp(end_log)
    move = jnp.where(row == col, end, 0.0) - left[:, :LANES]
    query = queries.astype(F32) * growth_col - read[:, :LANES]
    return query, read[:, LANES:], move, left[:, LANES:]


def kernel(
    ranks, members, heads,
    q_ref, k_ref, v_ref, gate_ref,
    out_ref,
    q_in, k_in, v_in, gate_in, cum, cum_t, beta_t, state_in, state_out, read_map, read_base, staged,
    gate_send, gate_recv, part_send, part_recv, own_sem,
    state_send, state_recv, out_send, out_recv, own_out,
):
    rank, member = lax.axis_index("seq"), lax.axis_index("head")
    following, leading = lax.rem(rank + 1, ranks), lax.rem(rank + ranks - 1, ranks)
    sources, parts = (q_ref, k_ref, v_ref), (q_in, k_in, v_in)

    barrier = pltpu.get_barrier_semaphore()
    for away in range(1, members):
        pl.semaphore_signal(
            barrier, inc=1, device_id=(rank, lax.rem(member + away, members)), device_id_type=MESH
        )
    for other in (following, leading):
        pl.semaphore_signal(barrier, inc=1, device_id=(other, member), device_id_type=MESH)
    pl.semaphore_wait(barrier, members + 1)

    def columns(owner, i):
        return pl.ds(pl.multiple_of((owner * heads + i) * LANES, LANES), LANES)

    def gate_copy(away):
        target = lax.rem(member + away, members)
        return pltpu.make_async_remote_copy(
            src_ref=gate_ref.at[target], dst_ref=gate_in.at[member],
            send_sem=gate_send.at[away], recv_sem=gate_recv.at[away],
            device_id=(rank, target), device_id_type=MESH,
        )

    def part_copy(i, away, a):
        target = lax.rem(member + away, members)
        return pltpu.make_async_remote_copy(
            src_ref=sources[a].at[:, columns(target, i)], dst_ref=parts[a].at[i, member],
            send_sem=part_send.at[i, away, a], recv_sem=part_recv.at[i, away, a],
            device_id=(rank, target), device_id_type=MESH,
        )

    def part_arrival(i, away, a):
        origin = lax.rem(member + members - away, members)
        return pltpu.make_async_remote_copy(
            src_ref=sources[a].at[:, columns(origin, i)], dst_ref=parts[a].at[i, origin],
            send_sem=part_send.at[i, away, a], recv_sem=part_recv.at[i, away, a],
            device_id=(rank, origin), device_id_type=MESH,
        )

    def own_copy(i, a):
        return pltpu.make_async_copy(
            sources[a].at[:, columns(member, i)], parts[a].at[i, member], own_sem.at[i, a]
        )

    def state_copy(i):
        return pltpu.make_async_remote_copy(
            src_ref=state_out.at[i], dst_ref=state_in.at[i],
            send_sem=state_send.at[i], recv_sem=state_recv.at[i],
            device_id=(following, member), device_id_type=MESH,
        )

    def out_copy(i, away):
        target = lax.rem(member + away, members)
        return pltpu.make_async_remote_copy(
            src_ref=staged.at[i, target], dst_ref=out_ref.at[:, columns(member, i)],
            send_sem=out_send.at[i, away], recv_sem=out_recv.at[i, away],
            device_id=(rank, target), device_id_type=MESH,
        )

    def out_arrival(i, away):
        origin = lax.rem(member + members - away, members)
        return pltpu.make_async_remote_copy(
            src_ref=staged.at[i, origin], dst_ref=out_ref.at[:, columns(origin, i)],
            send_sem=out_send.at[i, away], recv_sem=out_recv.at[i, away],
            device_id=(rank, origin), device_id_type=MESH,
        )

    def own_out_copy(i):
        return pltpu.make_async_copy(
            staged.at[i, member], out_ref.at[:, columns(member, i)], own_out.at[i]
        )

    own_gate = pltpu.make_async_copy(gate_ref.at[member], gate_in.at[member], gate_recv.at[0])
    own_gate.start()
    for away in range(1, members):
        gate_copy(away).start()

    @pl.loop(0, heads)
    def _(i):
        for a in (1, 0, 2):
            for away in range(1, members):
                part_copy(i, away, a).start()
            own_copy(i, a).start()

    row = lax.broadcasted_iota(jnp.int32, (LANES, LANES), 0)
    col = lax.broadcasted_iota(jnp.int32, (LANES, LANES), 1)
    own_gate.wait()
    for away in range(1, members):
        gate_copy(away).wait()
    until = jnp.where(row >= col, 1.0, 0.0).astype(BF16)
    until_t = jnp.where(row <= col, 1.0, 0.0).astype(BF16)
    for b in range(members):
        cum[b] = dot(until, gate_in[b, 0])
        cum_t[b] = dot(gate_in[b, 1], until_t)
        beta_t[b] = gate_in[b, 1].astype(F32)

    @pl.loop(0, heads)
    def _(i):
        for a in range(3):
            for away in range(1, members):
                part_arrival(i, away, a).wait_recv()
            own_copy(i, a).wait()
        maps = []
        for b in range(members):
            beta_col = jnp.sum(
                jnp.where(col == i, gate_in[b, 0].astype(F32), 0.0), axis=1, keepdims=True
            )
            cum_col = jnp.sum(jnp.where(col == heads + i, cum[b], 0.0), axis=1, keepdims=True)
            maps.append(
                block_maps(
                    k_in[i, b], q_in[i, b], v_in[i, b],
                    beta_col, beta_t[b, pl.ds(i, 1), :],
                    cum_col, cum_t[b, pl.ds(heads + i, 1), :], row, col,
                )
            )
        query, output, move, left = maps[0]
        read_map[0], read_base[0] = query, output
        moved = jnp.concatenate([move, left], axis=1)
        for b in range(1, members):
            query, output, move, left = maps[b]
            both = dot3(jnp.concatenate([move, query], axis=0), moved)
            read_map[b] = both[LANES:, :LANES]
            read_base[b] = both[LANES:, LANES:] + output
            moved = jnp.concatenate([both[:LANES, :LANES], both[:LANES, LANES:] + left], axis=1)
        total_map, total_base = left3(moved[:, :LANES]), moved[:, LANES:]

        @pl.when(rank > 0)
        def _():
            state_copy(i).wait_recv()

        @pl.when(rank == 0)
        def _():
            state_in[i] = jnp.zeros((LANES, LANES), F32)

        entering = right3(state_in[i])
        state_out[i] = total_base + dot(total_map, entering)

        @pl.when(rank < ranks - 1)
        def _():
            state_copy(i).start()

        for b in range(members):
            staged[i, b] = (read_base[b] + dot(left3(read_map[b]), entering)).astype(BF16)
        for away in range(1, members):
            out_copy(i, away).start()
        own_out_copy(i).start()

    @pl.loop(0, heads)
    def _(i):
        for away in range(1, members):
            for a in range(3):
                part_copy(i, away, a).wait_send()
            out_copy(i, away).wait_send()
            out_arrival(i, away).wait_recv()
        own_out_copy(i).wait()

        @pl.when(rank < ranks - 1)
        def _():
            state_copy(i).wait_send()


def shards(ranks, members, query_rows, key_rows, value_rows, write_rate, log_decay):
    tokens, all_heads = write_rate.shape
    heads = all_heads // members
    both = jnp.stack(
        [write_rate.reshape(tokens, members, heads), log_decay.reshape(tokens, members, heads)], axis=2
    ).reshape(tokens, members, 2 * heads)
    both = jnp.pad(jnp.swapaxes(both, 0, 1), ((0, 0), (0, 0), (0, LANES - 2 * heads)))
    gates = jnp.stack([both, jnp.swapaxes(both, 1, 2)], axis=1)
    anywhere = pl.BlockSpec(memory_space=pl.ANY)
    part = pltpu.VMEM((heads, members, tokens, LANES), BF16)
    square = pltpu.VMEM((members, LANES, LANES), F32)
    state = pltpu.VMEM((heads, LANES, LANES), F32)
    dma = pltpu.SemaphoreType.DMA
    return pl.pallas_call(
        functools.partial(kernel, ranks, members, heads),
        out_shape=jax.ShapeDtypeStruct(value_rows.shape, BF16),
        in_specs=[anywhere] * 4,
        out_specs=anywhere,
        scratch_shapes=[
            part, part, part,
            pltpu.VMEM((members, 2, LANES, LANES), BF16),
            square, square, square,
            state, state,
            square, square,
            part,
            dma((members,)), dma((members,)),
            dma((heads, members, 3)), dma((heads, members, 3)), dma((heads, 3)),
            dma((heads,)), dma((heads,)),
            dma((heads, members)), dma((heads, members)), dma((heads,)),
        ],
        compiler_params=pltpu.CompilerParams(
            collective_id=0, has_side_effects=True, vmem_limit_bytes=40 * 1024 * 1024
        ),
        cost_estimate=pl.CostEstimate(flops=10**10, bytes_accessed=2**23, transcendentals=0),
    )(query_rows, key_rows, value_rows, gates)


def solution(mesh):
    placed = P(("seq", "head"), None)
    return jax.shard_map(
        functools.partial(shards, mesh.shape["seq"], mesh.shape["head"]),
        mesh=mesh, in_specs=(placed,) * 5, out_specs=placed, check_vma=False,
    )
```

profile of v0, /device:TPU:27, one launch (start us, length us, event | category | flops | bytes accessed | tf_op | source)
XLA Modules:
  0.0 134.2 jit_solution(9830761900414955927)
XLA Ops:
  0.0 0.0 copy-start
  0.0 0.8 maximum_bitcast_fusion
  0.9 0.1 copy.8
  1.0 0.2 copy-done
  1.3 0.0 copy-start.1
  1.3 1.2 copy-done.1
  2.5 0.0 copy-start.2
  2.5 1.2 copy-done.2
  3.7 129.5 %shard_map.55 = bf16[128,4096]{1,0:T(8,128)(2,1)S(1)} custom-call(bf16[128,4096]{1,0:T(8,128)(2,1)S(1)} %copy-done, bf16[128,4096]{1,0:T(8,128)(2,1)S(1)} %copy-done.1, bf16[128,4096]{1,0:T(8,128)(2,1)S(1)} %copy-done.2, bf16[4,2,128,128]{3,2,1,0:T(8,128)(2,1)S(1)} %pad_maximum_fusion.gate_ref), custom_call_target="tpu_custom_call" | custom-call | flops 10000000000 | bytes 8388608 | tf_op jit(solution)/shard_map/pallas_call | solution.py:267
  133.2 1.0 copy.10
  (2 shorter events, 0.1 us)
Async XLA Ops:
  0.0 1.3 copy-start
  1.3 1.2 copy-start.1
  2.5 1.2 copy-start.2
where the time goes:
time: 134 us
  Pallas kernels  130 us (97%)
  local copies, waits for them, and re-layouts  3.83 us (3%)
    pallas_call x1, Pallas kernels, shards(): pl.pallas_call(functools.partial(kernel, ranks, members, heads), out_shap...  130 us
    unnamed x7, local copies, waits for them, and re-layouts  3.66 us

commit v1 on v0

--- a/solution.py
+++ b/solution.py
@@ -41,44 +41,107 @@
     return dot(left3(a), right3(b))
 
 
-def block_maps(keys, queries, values, beta_col, beta_row, cum_col, cum_row, row, col):
-    gram = dot_t(keys, keys, ((1,), (1,)))
-    raw_scores = dot_t(queries, keys, ((1,), (1,)))
-    diagonal = jnp.where(row == col, gram, 0.0)
-    r_col = lax.rsqrt(jnp.sum(diagonal, axis=1, keepdims=True) + EPSILON)
-    r_row = lax.rsqrt(jnp.sum(diagonal, axis=0, keepdims=True) + EPSILON)
-    within = row >= col
-    ratios = jnp.where(within, jnp.exp(jnp.where(within, cum_col - cum_row, 0.0)), 0.0)
-    faded = ratios * r_row
-    lower = jnp.where(row > col, gram * faded * (beta_col * r_col), 0.0)
-    scores = raw_scores * faded
+def blockwise(compact, row, col, size):
+    whole = jnp.concatenate([compact] * (LANES // size), axis=0)
+    return jnp.where((row ^ col) < size, whole, 0.0)
+
+
+def side_by_side(matrix, size):
+    return functools.reduce(jnp.add, [matrix[at : at + size] for at in range(0, LANES, size)])
+
+
+def unit_lower_inverses(lowers, row, col):
     apart = row ^ col
-    inverse = jnp.where(row == col, 1.0, 0.0) - jnp.where(apart == 1, lower, 0.0)
+    small = 32
+
+    def corner(lower, span):
+        return jnp.where((apart >= span) & (apart < 2 * span), lower, 0.0)
+
+    unit = jnp.where(row == col, 1.0, 0.0)
+    found = [unit - corner(lower, 1) for lower in lowers]
+    packed = [side_by_side(x, small) for x in found]
     span = 2
+    while span < small:
+        corners = [side_by_side(corner(lower, span), small) for lower in lowers]
+        whole = [right3(blockwise(x, row, col, small)) for x in packed]
+        partial = [dot(left3(c), w) for c, w in zip(corners, whole)]
+        whole = [right3(blockwise(x, row, col, small)) for x in partial]
+        packed = [x - dot(left3(x), w) for x, w in zip(packed, whole)]
+        span *= 2
+    found = [blockwise(x, row, col, small) for x in packed]
     while span < LANES:
-        corner = jnp.where((apart >= span) & (apart < 2 * span), lower, 0.0)
-        partial = dot3(corner, inverse)
-        inverse = inverse - dot3(inverse, partial)
+        odd = range(span, LANES, 2 * span)
+        lefts = [
+            left3(jnp.concatenate([corner(lower, span)[at : at + span] for at in odd], axis=0))
+            for lower in lowers
+        ]
+        partial = [dot(c, right3(x)) for c, x in zip(lefts, found)]
+        nothing = jnp.zeros((span, LANES), F32)
+        spread = [
+            right3(
+                jnp.concatenate(
+                    [
+                        piece
+                        for n in range(len(odd))
+                        for piece in (nothing, x[n * span : (n + 1) * span])
+                    ],
+                    axis=0,
+                )
+            )
+            for x in partial
+        ]
+        lefts = [left3(jnp.concatenate([x[at : at + span] for at in odd], axis=0)) for x in found]
+        change = [dot(x, w) for x, w in zip(lefts, spread)]
+        found = [
+            jnp.concatenate(
+                [
+                    piece
+                    for n, at in enumerate(odd)
+                    for piece in (
+                        x[at - span : at], x[at : at + span] - c[n * span : (n + 1) * span]
+                    )
+                ],
+                axis=0,
+            )
+            for x, c in zip(found, change)
+        ]
         span *= 2
-    growth_col = jnp.exp(cum_col)
-    growth_row = jnp.exp(cum_row)
-    end_log = cum_row[:, LANES - 1 :]
-    for_values = jnp.concatenate(halves(inverse * beta_row), axis=1)
-    for_keys = jnp.concatenate(halves(inverse * (beta_row * growth_row * r_row)), axis=1)
-    base = dot(for_values, jnp.concatenate([values, values], axis=0))
-    wy = dot(for_keys, jnp.concatenate([keys, keys], axis=0))
-    solved = jnp.concatenate([wy, base], axis=1)
-    read = dot3(scores, solved)
-    carried = solved * (r_col * jnp.exp(end_log - cum_col))
-    left = dot_t(
-        jnp.concatenate([keys, keys], axis=0),
-        jnp.concatenate(halves(carried), axis=0),
-        ((0,), (0,)),
-    )
-    end = jnp.exp(end_log)
-    move = jnp.where(row == col, end, 0.0) - left[:, :LANES]
-    query = queries.astype(F32) * growth_col - read[:, :LANES]
-    return query, read[:, LANES:], move, left[:, LANES:]
+    return found
+
+
+def block_maps(units, row, col):
+    prepared = []
+    for keys, queries, values, beta_col, beta_row, cum_col, cum_row in units:
+        keys_t = keys.T
+        products = dot(jnp.concatenate([keys, queries], axis=0), keys_t)
+        gram, raw_scores = products[:LANES], products[LANES:]
+        diagonal = jnp.where(row == col, gram, 0.0)
+        r_col = lax.rsqrt(jnp.sum(diagonal, axis=1, keepdims=True) + EPSILON)
+        r_row = lax.rsqrt(jnp.sum(diagonal, axis=0, keepdims=True) + EPSILON)
+        within = row >= col
+        ratios = jnp.where(within, jnp.exp(jnp.where(within, cum_col - cum_row, 0.0)), 0.0)
+        faded = ratios * r_row
+        lower = jnp.where(row > col, gram * faded * (beta_col * r_col), 0.0)
+        prepared.append((keys_t, lower, raw_scores * faded, r_col, r_row))
+    inverses = unit_lower_inverses([p[1] for p in prepared], row, col)
+    maps = []
+    for unit, (keys_t, _, scores, r_col, r_row), inverse in zip(units, prepared, inverses):
+        keys, queries, values, _, beta_row, cum_col, cum_row = unit
+        end_log = cum_row[:, LANES - 1 :]
+        for_values = jnp.concatenate(halves(inverse * beta_row), axis=1)
+        for_keys = jnp.concatenate(halves(inverse * (beta_row * jnp.exp(cum_row) * r_row)), axis=1)
+        base = dot(for_values, jnp.concatenate([values, values], axis=0))
+        wy = dot(for_keys, jnp.concatenate([keys, keys], axis=0))
+        solved = jnp.concatenate([wy, base], axis=1)
+        read = dot3(scores, solved)
+        carried = solved * (r_col * jnp.exp(end_log - cum_col))
+        left = dot(
+            jnp.concatenate([keys_t, keys_t], axis=1), jnp.concatenate(halves(carried), axis=0)
+        )
+        move = jnp.where(row == col, jnp.exp(end_log), 0.0) - left[:, :LANES]
+        query = queries.astype(F32) * jnp.exp(cum_col) - read[:, :LANES]
+        maps.append((query, read[:, LANES:], move, left[:, LANES:]))
+    return maps
 
 
 def kernel(
@@ -192,19 +255,20 @@
             for away in range(1, members):
                 part_arrival(i, away, a).wait_recv()
             own_copy(i, a).wait()
-        maps = []
+        units = []
         for b in range(members):
             beta_col = jnp.sum(
                 jnp.where(col == i, gate_in[b, 0].astype(F32), 0.0), axis=1, keepdims=True
             )
             cum_col = jnp.sum(jnp.where(col == heads + i, cum[b], 0.0), axis=1, keepdims=True)
-            maps.append(
-                block_maps(
+            units.append(
+                (
                     k_in[i, b], q_in[i, b], v_in[i, b],
                     beta_col, beta_t[b, pl.ds(i, 1), :],
-                    cum_col, cum_t[b, pl.ds(heads + i, 1), :], row, col,
+                    cum_col, cum_t[b, pl.ds(heads + i, 1), :],
                 )
             )
+        maps = block_maps(units, row, col)
         query, output, move, left = maps[0]
         read_map[0], read_base[0] = query, output
         moved = jnp.concatenate([move, left], axis=1)
@@ -231,8 +295,9 @@
         def _():
             state_copy(i).start()
 
-        for b in range(members):
-            staged[i, b] = (read_base[b] + dot(left3(read_map[b]), entering)).astype(BF16)
+        reading = left3(read_map[...].reshape(members * LANES, LANES))
+        reached = read_base[...] + dot(reading, entering).reshape(members, LANES, LANES)
+        staged[i] = reached.astype(BF16)
         for away in range(1, members):
             out_copy(i, away).start()
         own_out_copy(i).start()
@@ -282,7 +347,7 @@
             dma((heads, members)), dma((heads, members)), dma((heads,)),
         ],
         compiler_params=pltpu.CompilerParams(
-            collective_id=0, has_side_effects=True, vmem_limit_bytes=40 * 1024 * 1024
+            collective_id=0, has_side_effects=True, vmem_limit_bytes=60 * 1024 * 1024
         ),
         cost_estimate=pl.CostEstimate(flops=10**10, bytes_accessed=2**23, transcendentals=0),
     )(query_rows, key_rows, value_rows, gates)

time: 134 us -> 83.4 us (0.62)
  Pallas kernels: 130 us -> 79.2 us
  local copies, waits for them, and re-layouts: 3.83 us -> 2.46 us
    pallas_call x1, Pallas kernels: 130 us -> 79.2 us  [shards(): pl.pallas_call(functools.partial(kernel, ranks, members, heads), out_shap...]
    unnamed x7 -> x1, local copies, waits for them, and re-layouts: 3.66 us -> 2.29 us
where the time goes in v1:
time: 83.4 us; the launch traced here: 83.1 us
  Pallas kernels  79.2 us (95%)
  local copies, waits for them, and re-layouts  2.46 us (3%)
  other arithmetic  1.45 us (2%)
    pallas_call x1, Pallas kernels, shards(): pl.pallas_call(functools.partial(kernel, ranks, members, heads), out_shap...  79.2 us
    unnamed x1, local copies, waits for them, and re-layouts  2.29 us

profile of v1, /device:TPU:27, one launch (start us, length us, event | category | flops | bytes accessed | tf_op | source)
XLA Modules:
  0.0 83.1 jit_solution(18253908525254462253)
XLA Ops:
  0.0 0.7 maximum_bitcast_fusion
  0.8 0.1 copy.8
  0.9 0.7 pad_maximum_fusion.gate_ref
  1.6 79.2 %shard_map.55 = bf16[128,4096]{1,0:T(8,128)(2,1)} custom-call(bf16[128,4096]{1,0:T(8,128)(2,1)} %q_ref.1, bf16[128,4096]{1,0:T(8,128)(2,1)} %k_ref.1, bf16[128,4096]{1,0:T(8,128)(2,1)} %v_ref.1, bf16[4,2,128,128]{3,2,1,0:T(8,128)(2,1)} %pad_maximum_fusion.gate_ref), custom_call_target="tpu_custom_call" | custom-call | flops 10000000000 | bytes 8388608 | tf_op jit(solution)/shard_map/pallas_call | solution.py:332
  80.8 2.3 %copy.10 = bf16[128,4096]{1,0:T(8,128)(2,1)} copy(bf16[128,4096]{1,0:T(8,128)(2,1)} %shard_map.55) | data formatting | bytes 2097152
  (1 shorter events, 0.0 us)

commit v2 on v1

--- a/solution.py
+++ b/solution.py
@@ -109,46 +109,46 @@
     return found
 
 
-def block_maps(units, row, col):
+def fading(cum_col, cum_row, r_row, row, col):
+    within = row >= col
+    return jnp.where(within, jnp.exp(jnp.where(within, cum_col - cum_row, 0.0)), 0.0) * r_row
+
+
+def block_moves(units, row, col):
     prepared = []
-    for keys, queries, values, beta_col, beta_row, cum_col, cum_row in units:
+    for keys, values, beta_col, beta_row, cum_col, cum_row in units:
         keys_t = keys.T
-        products = dot(jnp.concatenate([keys, queries], axis=0), keys_t)
-        gram, raw_scores = products[:LANES], products[LANES:]
+        gram = dot(keys, keys_t)
         diagonal = jnp.where(row == col, gram, 0.0)
         r_col = lax.rsqrt(jnp.sum(diagonal, axis=1, keepdims=True) + EPSILON)
         r_row = lax.rsqrt(jnp.sum(diagonal, axis=0, keepdims=True) + EPSILON)
-        within = row >= col
-        ratios = jnp.where(within, jnp.exp(jnp.where(within, cum_col - cum_row, 0.0)), 0.0)
-        faded = ratios * r_row
+        faded = fading(cum_col, cum_row, r_row, row, col)
         lower = jnp.where(row > col, gram * faded * (beta_col * r_col), 0.0)
-        prepared.append((keys_t, lower, raw_scores * faded, r_col, r_row))
+        prepared.append((keys_t, lower, r_col, r_row))
     inverses = unit_lower_inverses([p[1] for p in prepared], row, col)
-    maps = []
-    for unit, (keys_t, _, scores, r_col, r_row), inverse in zip(units, prepared, inverses):
-        keys, queries, values, _, beta_row, cum_col, cum_row = unit
+    moves = []
+    for unit, (keys_t, _, r_col, r_row), inverse in zip(units, prepared, inverses):
+        keys, values, _, beta_row, cum_col, cum_row = unit
         end_log = cum_row[:, LANES - 1 :]
         for_values = jnp.concatenate(halves(inverse * beta_row), axis=1)
         for_keys = jnp.concatenate(halves(inverse * (beta_row * jnp.exp(cum_row) * r_row)), axis=1)
         base = dot(for_values, jnp.concatenate([values, values], axis=0))
         wy = dot(for_keys, jnp.concatenate([keys, keys], axis=0))
         solved = jnp.concatenate([wy, base], axis=1)
-        read = dot3(scores, solved)
         carried = solved * (r_col * jnp.exp(end_log - cum_col))
         left = dot(
             jnp.concatenate([keys_t, keys_t], axis=1), jnp.concatenate(halves(carried), axis=0)
         )
         move = jnp.where(row == col, jnp.exp(end_log), 0.0) - left[:, :LANES]
-        query = queries.astype(F32) * jnp.exp(cum_col) - read[:, :LANES]
-        maps.append((query, read[:, LANES:], move, left[:, LANES:]))
-    return maps
+        moves.append((solved, r_row, move, left[:, LANES:]))
+    return moves
 
 
 def kernel(
     ranks, members, heads,
     q_ref, k_ref, v_ref, gate_ref,
     out_ref,
-    q_in, k_in, v_in, gate_in, cum, cum_t, beta_t, state_in, state_out, read_map, read_base, staged,
+    q_in, k_in, v_in, gate_in, cum, cum_t, beta_t, state_in, state_out, solutions, norms, moved_in, staged,
     gate_send, gate_recv, part_send, part_recv, own_sem,
     state_send, state_recv, out_send, out_recv, own_out,
 ):
@@ -232,10 +232,16 @@
 
     @pl.loop(0, heads)
     def _(i):
-        for a in (1, 0, 2):
+        for a in (1, 2):
             for away in range(1, members):
                 part_copy(i, away, a).start()
             own_copy(i, a).start()
+
+    @pl.loop(0, heads)
+    def _(i):
+        for away in range(1, members):
+            part_copy(i, away, 0).start()
+        own_copy(i, 0).start()
 
     row = lax.broadcasted_iota(jnp.int32, (LANES, LANES), 0)
     col = lax.broadcasted_iota(jnp.int32, (LANES, LANES), 1)
@@ -249,55 +255,79 @@
         cum_t[b] = dot(gate_in[b, 1], until_t)
         beta_t[b] = gate_in[b, 1].astype(F32)
 
-    @pl.loop(0, heads)
-    def _(i):
-        for a in range(3):
+    def decays(i, b):
+        cum_col = jnp.sum(jnp.where(col == heads + i, cum[b], 0.0), axis=1, keepdims=True)
+        return cum_col, cum_t[b, pl.ds(heads + i, 1), :]
+
+    def arrived(i, arrays):
+        for a in arrays:
             for away in range(1, members):
                 part_arrival(i, away, a).wait_recv()
             own_copy(i, a).wait()
+
+    def pass_on(i):
+        @pl.when(rank > 0)
+        def _():
+            state_copy(i).wait_recv()
+
+        @pl.when(rank == 0)
+        def _():
+            state_in[i] = jnp.zeros((LANES, LANES), F32)
+
+        @pl.when(rank < ranks - 1)
+        def _():
+            total = moved_in[i, members - 1]
+            state_out[i] = total[:, LANES:] + dot3(total[:, :LANES], state_in[i])
+            state_copy(i).start()
+
+    late = jnp.minimum(rank, heads)
+
+    @pl.loop(0, heads)
+    def _(i):
+        arrived(i, (1, 2))
         units = []
         for b in range(members):
             beta_col = jnp.sum(
                 jnp.where(col == i, gate_in[b, 0].astype(F32), 0.0), axis=1, keepdims=True
             )
-            cum_col = jnp.sum(jnp.where(col == heads + i, cum[b], 0.0), axis=1, keepdims=True)
             units.append(
-                (
-                    k_in[i, b], q_in[i, b], v_in[i, b],
-                    beta_col, beta_t[b, pl.ds(i, 1), :],
-                    cum_col, cum_t[b, pl.ds(heads + i, 1), :],
-                )
+                (k_in[i, b], v_in[i, b], beta_col, beta_t[b, pl.ds(i, 1), :], *decays(i, b))
             )
-        maps = block_maps(units, row, col)
-        query, output, move, left = maps[0]
-        read_map[0], read_base[0] = query, output
-        moved = jnp.concatenate([move, left], axis=1)
-        for b in range(1, members):
-            query, output, move, left = maps[b]
-            both = dot3(jnp.concatenate([move, query], axis=0), moved)
-            read_map[b] = both[LANES:, :LANES]
-            read_base[b] = both[LANES:, LANES:] + output
-            moved = jnp.concatenate([both[:LANES, :LANES], both[:LANES, LANES:] + left], axis=1)
-        total_map, total_base = left3(moved[:, :LANES]), moved[:, LANES:]
-
-        @pl.when(rank > 0)
-        def _():
-            state_copy(i).wait_recv()
-
-        @pl.when(rank == 0)
-        def _():
-            state_in[i] = jnp.zeros((LANES, LANES), F32)
-
-        entering = right3(state_in[i])
-        state_out[i] = total_base + dot(total_map, entering)
-
-        @pl.when(rank < ranks - 1)
-        def _():
-            state_copy(i).start()
-
-        reading = left3(read_map[...].reshape(members * LANES, LANES))
-        reached = read_base[...] + dot(reading, entering).reshape(members, LANES, LANES)
-        staged[i] = reached.astype(BF16)
+        moves = block_moves(units, row, col)
+        moved = None
+        for b, (solved, r_row, move, left) in enumerate(moves):
+            solutions[i, b] = solved
+            norms[i, b] = jnp.broadcast_to(r_row, (8, LANES))
+            if moved is None:
+                moved = jnp.concatenate([move, left], axis=1)
+            else:
+                both = dot3(move, moved)
+                moved = jnp.concatenate([both[:, :LANES], both[:, LANES:] + left], axis=1)
+            moved_in[i, b] = moved
+
+        @pl.when(i >= late)
+        def _():
+            pass_on(i - late)
+
+    @pl.loop(0, heads)
+    def _(i):
+        @pl.when(i < late)
+        def _():
+            pass_on(heads + i - late)
+
+        arrived(i, (0,))
+        entering = state_in[i]
+        before = moved_in[i, : members - 1].reshape((members - 1) * LANES, 2 * LANES)
+        later = dot(left3(before[:, :LANES]), right3(entering)) + before[:, LANES:]
+        for b in range(members):
+            cum_col, cum_row = decays(i, b)
+            queries = q_in[i, b]
+            faded = fading(cum_col, cum_row, norms[i, b, :1, :], row, col)
+            scores = dot_t(queries, k_in[i, b], ((1,), (1,))) * faded
+            read = dot3(scores, solutions[i, b])
+            query = queries.astype(F32) * jnp.exp(cum_col) - read[:, :LANES]
+            state = entering if b == 0 else later[(b - 1) * LANES : b * LANES]
+            staged[i, b] = (read[:, LANES:] + dot3(query, state)).astype(BF16)
         for away in range(1, members):
             out_copy(i, away).start()
         own_out_copy(i).start()
@@ -339,7 +369,9 @@
             pltpu.VMEM((members, 2, LANES, LANES), BF16),
             square, square, square,
             state, state,
-            square, square,
+            pltpu.VMEM((heads, members, LANES, 2 * LANES), F32),
+            pltpu.VMEM((heads, members, 8, LANES), F32),
+            pltpu.VMEM((heads, members, LANES, 2 * LANES), F32),
             part,
             dma((members,)), dma((members,)),
             dma((heads, members, 3)), dma((heads, members, 3)), dma((heads, 3)),

time: 83.4 us -> 77.7 us (0.932)
  Pallas kernels: 79.2 us -> 73.5 us
    pallas_call x1, Pallas kernels: 79.2 us -> 73.5 us  [shards(): pl.pallas_call(functools.partial(kernel, ranks, members, heads), out_shap...]
where the time goes in v2:
time: 77.7 us; the launch traced here: 77.5 us
  Pallas kernels  73.5 us (95%)
  local copies, waits for them, and re-layouts  2.46 us (3%)
  other arithmetic  1.45 us (2%)
    pallas_call x1, Pallas kernels, shards(): pl.pallas_call(functools.partial(kernel, ranks, members, heads), out_shap...  73.5 us
    unnamed x1, local copies, waits for them, and re-layouts  2.29 us

profile of v2, /device:TPU:27, one launch (start us, length us, event | category | flops | bytes accessed | tf_op | source)
XLA Modules:
  0.0 77.5 jit_solution(4435784825341476432)
XLA Ops:
  0.0 0.7 maximum_bitcast_fusion
  0.8 0.1 copy.8
  0.9 0.7 pad_maximum_fusion.gate_ref
  1.6 73.5 %shard_map.55 = bf16[128,4096]{1,0:T(8,128)(2,1)} custom-call(bf16[128,4096]{1,0:T(8,128)(2,1)} %q_ref.1, bf16[128,4096]{1,0:T(8,128)(2,1)} %k_ref.1, bf16[128,4096]{1,0:T(8,128)(2,1)} %v_ref.1, bf16[4,2,128,128]{3,2,1,0:T(8,128)(2,1)} %pad_maximum_fusion.gate_ref), custom_call_target="tpu_custom_call" | custom-call | flops 10000000000 | bytes 8388608 | tf_op jit(solution)/shard_map/pallas_call | solution.py:362
  75.2 2.3 %copy.10 = bf16[128,4096]{1,0:T(8,128)(2,1)} copy(bf16[128,4096]{1,0:T(8,128)(2,1)} %shard_map.55) | data formatting | bytes 2097152
  (1 shorter events, 0.0 us)

commit v3 on v2

--- a/solution.py
+++ b/solution.py
@@ -266,6 +266,9 @@
             own_copy(i, a).wait()
 
     def pass_on(i):
+        total = moved_in[i, members - 1]
+        total_map = left3(total[:, :LANES])
+
         @pl.when(rank > 0)
         def _():
             state_copy(i).wait_recv()
@@ -276,8 +279,7 @@
 
         @pl.when(rank < ranks - 1)
         def _():
-            total = moved_in[i, members - 1]
-            state_out[i] = total[:, LANES:] + dot3(total[:, :LANES], state_in[i])
+            state_out[i] = total[:, LANES:] + dot(total_map, right3(state_in[i]))
             state_copy(i).start()
 
     late = jnp.minimum(rank, heads)
@@ -363,7 +365,7 @@
         functools.partial(kernel, ranks, members, heads),
         out_shape=jax.ShapeDtypeStruct(value_rows.shape, BF16),
         in_specs=[anywhere] * 4,
-        out_specs=anywhere,
+        out_specs=pl.BlockSpec(memory_space=pltpu.VMEM),
         scratch_shapes=[
             part, part, part,
             pltpu.VMEM((members, 2, LANES, LANES), BF16),

time: 77.7 us -> 78.7 us (1.013)
  Pallas kernels: 73.5 us -> 74.5 us
    pallas_call x1, Pallas kernels: 73.5 us -> 74.5 us  [shards(): pl.pallas_call(functools.partial(kernel, ranks, members, heads), out_shap...]
where the time goes in v3:
time: 78.7 us; the launch traced here: 78.4 us
  Pallas kernels  74.5 us (95%)
  local copies, waits for them, and re-layouts  2.46 us (3%)
  other arithmetic  1.45 us (2%)
    pallas_call x1, Pallas kernels, shards(): pl.pallas_call(functools.partial(kernel, ranks, members, heads), out_shap...  74.5 us
    unnamed x1, local copies, waits for them, and re-layouts  2.29 us

profile of v3, /device:TPU:27, one launch (start us, length us, event | category | flops | bytes accessed | tf_op | source)
XLA Modules:
  0.0 78.4 jit_solution(320879693010314560)
XLA Ops:
  0.0 0.7 maximum_bitcast_fusion
  0.8 0.1 copy.8
  0.9 0.7 pad_maximum_fusion.gate_ref
  1.6 74.5 %shard_map.55 = bf16[128,4096]{1,0:T(8,128)(2,1)} custom-call(bf16[128,4096]{1,0:T(8,128)(2,1)} %q_ref.1, bf16[128,4096]{1,0:T(8,128)(2,1)} %k_ref.1, bf16[128,4096]{1,0:T(8,128)(2,1)} %v_ref.1, bf16[4,2,128,128]{3,2,1,0:T(8,128)(2,1)} %pad_maximum_fusion.gate_ref), custom_call_target="tpu_custom_call" | custom-call | flops 10000000000 | bytes 8388608 | tf_op jit(solution)/shard_map/pallas_call | solution.py:364
  76.1 2.3 %copy.10 = bf16[128,4096]{1,0:T(8,128)(2,1)} copy(bf16[128,4096]{1,0:T(8,128)(2,1)} %shard_map.55) | data formatting | bytes 2097152
  (1 shorter events, 0.0 us)
